TPU v7x, 512 devices: a whole 4x4x16 slice. The times are simulated.
512 devices in a mesh: freq: 16 (over y, x), patch: 32 (over z, core).
Axes of the slice: x: 4, y: 4, z: 16, core: 2. Of those that a mesh axis runs over, the one named last changes fastest.
Arguments:
- responses: bfloat16 [2048, 2, 2048], P('patch', None, 'freq'), may hold values from -6 to 6
- adjoints: bfloat16 [2048, 2, 2048], P('patch', None, 'freq'), may hold values from -6 to 6
- patch_shapes: bfloat16 [3072, 4, 48, 128], P('patch'), may hold values from -0.25 to 0.25
- block_lists: int32 [3072, 4], P('patch'), may hold values from 0 to 15
- block_counts: int32 [3072], P('patch'), may hold values from 1 to 4
- patch_sizes: int32 [3072], P('patch'), may hold values from 12 to 48
- owner_map: int32 [3072], P('patch'), may hold values from 0 to 3071, each once
Outputs:
- loss_gradient: float32 [3072], P('patch')
Inputs may be any that keep to these rules, and one draw needn't show every extreme that they name: `owner_map`: each patch appears once.
All inputs are finite; a program needn't handle non-finite values.
Results may differ from a plain program's by a relative error of at most 0.0003.
Values may be sent and summed in bfloat16 or wider, within the bound.
A program may use at most 64 MiB of HBM per device.

v0:
```python
import math
import jax
import jax.numpy as jnp
from jax import lax
from jax.sharding import PartitionSpec as P


def strain_terms(total, masked, blocks, resp_piece, adjo_piece, width):
    count = resp_piece.shape[0]
    modes = resp_piece.shape[2]
    patches = masked.shape[0]
    samples = masked.shape[2]
    step = math.gcd(count, 32)
    turns = count // step

    def one(index, carry):
        resp = lax.dynamic_slice_in_dim(resp_piece, index * step, step, 0).reshape(
            step * 2, modes // width, width
        )
        adjo = lax.dynamic_slice_in_dim(adjo_piece, index * step, step, 0).reshape(
            step * 2, modes // width, width
        )
        forward = jnp.einsum(
            "pksb,cpkb->cps", masked, resp[:, blocks, :], preferred_element_type=jnp.float32
        )
        backward = jnp.einsum(
            "pksb,cpkb->cps", masked, adjo[:, blocks, :], preferred_element_type=jnp.float32
        )
        forward = forward.reshape(step, 2, patches, samples)
        backward = backward.reshape(step, 2, patches, samples)
        cross = forward[:, 0] * backward[:, 1] - forward[:, 1] * backward[:, 0]
        return carry + jnp.sum(cross, axis=(0, 2))

    return lax.fori_loop(0, turns, one, total)


def body(responses, adjoints, patch_shapes, block_lists, block_counts, patch_sizes, owner_map):
    patch_dev, slots, samples, width = patch_shapes.shape
    slot_live = jnp.arange(slots, dtype=jnp.int32)[None, :] < block_counts[:, None]
    row_live = jnp.arange(samples, dtype=jnp.int32)[None, :] < patch_sizes[:, None]
    live = (slot_live[:, :, None, None] & row_live[:, None, :, None]).astype(jnp.bfloat16)
    masked = patch_shapes * live
    freqs = responses.shape[0] * lax.axis_size("patch")
    empty = jnp.zeros((patch_dev,), jnp.float32)
    regrouped = (
        lax.all_to_all(responses, "freq", split_axis=0, concat_axis=2, tiled=True),
        lax.all_to_all(adjoints, "freq", split_axis=0, concat_axis=2, tiled=True),
    )
    terms = strain_terms(
        empty,
        masked,
        block_lists,
        lax.all_gather(regrouped[0], "patch", axis=0, tiled=True),
        lax.all_gather(regrouped[1], "patch", axis=0, tiled=True),
        width,
    )
    terms = terms * (samples * freqs) ** (-0.5)
    patches = patch_dev * lax.axis_size("patch")
    columns = jnp.arange(patches, dtype=jnp.int32)
    onehot = (owner_map[:, None] == columns[None, :]).astype(jnp.float32)
    dense = jnp.dot(terms, onehot, precision=lax.Precision.HIGHEST)
    mine = lax.psum_scatter(dense, "patch", scatter_dimension=0, tiled=True)
    return lax.psum(mine, "freq")


def solution(mesh):
    placed = (
        P("patch", None, "freq"),
        P("patch", None, "freq"),
        P("patch", None, None, None),
        P("patch", None),
        P("patch"),
        P("patch"),
        P("patch"),
    )
    return jax.shard_map(body, mesh=mesh, in_specs=placed, out_specs=P("patch"), check_vma=False)
```

profile of v0, /device:TPU:32, one launch (start us, length us, event | category | flops | bytes accessed | tf_op | source)
XLA Modules:
  0.0 486.1 jit_solution(6683167722934066681)
XLA Ops:
  6.5 14.6 %all_to_all.36 = bf16[64,2,128]{2,1,0:T(2,128)(2,1)S(1)} all-to-all(bf16[64,2,128]{2,1,0:T(2,128)(2,1)} %param.9), channel_id=1, replica_groups=mesh['freq'=16,'patch'=32] {'freq'}, dimensions={0} | all-to-all | bytes 65536 | tf_op jit(solution)/shard_map/all_to_all | solution.py:46
  21.9 11.0 %all_to_all.37 = bf16[64,2,128]{2,1,0:T(2,128)(2,1)S(1)} all-to-all(bf16[64,2,128]{2,1,0:T(2,128)(2,1)} %param.10), channel_id=1, replica_groups=mesh['freq'=16,'patch'=32] {'freq'}, dimensions={0} | all-to-all | bytes 65536 | tf_op jit(solution)/shard_map/all_to_all | solution.py:47
  38.0 6.3 %broadcast_multiply_fusion = bf16[96,4,48,128]{3,2,1,0:T(8,128)(2,1)} fusion(bf16[96,4,48,128]{3,2,1,0:T(8,128)(2,1)} %param.11, bf16[96,4,48]{2,1,0:T(4,128)(2,1)S(1)} %and_convert_fusion), kind=kLoop, calls=%fused_computation.14 | loop fusion | flops 2359296 | bytes 9474048 | tf_op jit(solution)/shard_map/mul | solution.py:42
  44.3 48.6 %all-gather.3.cloned.1.call-done = bf16[128,2,2048]{2,1,0:T(2,128)(2,1)} async-done(((bf16[4,2,2048]{2,1,0:T(2,128)(2,1)}), bf16[128,2,2048]{2,1,0:T(2,128)(2,1)}) %all-gather.3.cloned.1.call-update) | async-done | bytes 1048592 | tf_op jit(solution)/shard_map/all_gather | solution.py:53
  92.8 70.0 %all-gather.5.cloned.1.call-done = bf16[128,2,2048]{2,1,0:T(2,128)(2,1)} async-done(((bf16[4,2,2048]{2,1,0:T(2,128)(2,1)}), bf16[128,2,2048]{2,1,0:T(2,128)(2,1)}) %all-gather.5.cloned.1.call-update) | async-done | bytes 1048592 | tf_op jit(solution)/shard_map/all_gather | solution.py:54
  162.8 185.3 %while.14 = (s32[]{:T(128)}, f32[96]{0:T(128)S(1)}, bf16[128,2,2048]{2,1,0:T(2,128)(2,1)}, s32[96,4]{1,0:T(8,128)S(1)}, bf16[96,4,48,128]{3,2,1,0:T(8,128)(2,1)}...) while((s32[]{:T(128)}, f32[96]{0:T(128)S(1)}, ...), condition=%wide.region_2.0_spmd.clone, body=%wide.region_0.0_spmd.clone.sunk | while | flops 604571840 | bytes 59785376 | solution.py:34
  164.6 13.3 %gather_fusion = bf16[384,64,128]{2,1,0:T(8,128)(2,1)} fusion(bf16[64,16,128]{2,0,1:T(8,128)(2,1)S(1)} %copy.39, s32[1024]{0:T(1024)S(1)} %pad_clamp_fusion.2), kind=kCustom, calls=%fused_computation.1.clone.clone.1 | custom fusion | bytes 12584448 | tf_op jit(solution)/shard_map/while/body/eval_jaxpr/gather | solution.py:27
  177.9 5.9 %convolution_bitcast_fusion.4 = f32[64,96,48]{0,2,1:T(8,128)S(1)} fusion(bf16[64,96,4,128]{3,0,2,1:T(8,128)(2,1)} %bitcast.66, bf16[96,4,48,128]{3,2,1,0:T(8,128)(2,1)} %get-tuple-element.233), kind=kOutput, calls=%fused_computation.2.clone.1 | convolution fusion | flops 301989888 | bytes 12189696 | tf_op jit(solution)/shard_map/while/body/eval_jaxpr/pksb,cpkb->cps/dot_general | solution.py:26
  186.0 13.3 %gather_fusion.1 = bf16[384,64,128]{2,1,0:T(8,128)(2,1)} fusion(bf16[64,16,128]{2,0,1:T(8,128)(2,1)S(1)} %copy.41, s32[1024]{0:T(1024)S(1)} %pad_clamp_fusion.2), kind=kCustom, calls=%fused_computation.clone.clone.1 | custom fusion | bytes 12584448 | tf_op jit(solution)/shard_map/while/body/eval_jaxpr/gather | solution.py:24
  199.3 5.9 %convolution_bitcast_fusion.5 = f32[64,96,48]{0,2,1:T(8,128)S(1)} fusion(bf16[64,96,4,128]{3,0,2,1:T(8,128)(2,1)} %bitcast.65, bf16[96,4,48,128]{3,2,1,0:T(8,128)(2,1)} %get-tuple-element.233), kind=kOutput, calls=%fused_computation.3.clone.1 | convolution fusion | flops 301989888 | bytes 12189696 | tf_op jit(solution)/shard_map/while/body/eval_jaxpr/pksb,cpkb->cps/dot_general | solution.py:23
  210.9 13.3 %gather_fusion = bf16[384,64,128]{2,1,0:T(8,128)(2,1)} fusion(bf16[64,16,128]{2,0,1:T(8,128)(2,1)S(1)} %copy.39, s32[1024]{0:T(1024)S(1)} %pad_clamp_fusion.2), kind=kCustom, calls=%fused_computation.1.clone.clone.1 | custom fusion | bytes 12584448 | tf_op jit(solution)/shard_map/while/body/eval_jaxpr/gather | solution.py:27
  224.3 5.9 %convolution_bitcast_fusion.4 = f32[64,96,48]{0,2,1:T(8,128)S(1)} fusion(bf16[64,96,4,128]{3,0,2,1:T(8,128)(2,1)} %bitcast.66, bf16[96,4,48,128]{3,2,1,0:T(8,128)(2,1)} %get-tuple-element.233), kind=kOutput, calls=%fused_computation.2.clone.1 | convolution fusion | flops 301989888 | bytes 12189696 | tf_op jit(solution)/shard_map/while/body/eval_jaxpr/pksb,cpkb->cps/dot_general | solution.py:26
  232.3 13.3 %gather_fusion.1 = bf16[384,64,128]{2,1,0:T(8,128)(2,1)} fusion(bf16[64,16,128]{2,0,1:T(8,128)(2,1)S(1)} %copy.41, s32[1024]{0:T(1024)S(1)} %pad_clamp_fusion.2), kind=kCustom, calls=%fused_computation.clone.clone.1 | custom fusion | bytes 12584448 | tf_op jit(solution)/shard_map/while/body/eval_jaxpr/gather | solution.py:24
  245.6 5.9 %convolution_bitcast_fusion.5 = f32[64,96,48]{0,2,1:T(8,128)S(1)} fusion(bf16[64,96,4,128]{3,0,2,1:T(8,128)(2,1)} %bitcast.65, bf16[96,4,48,128]{3,2,1,0:T(8,128)(2,1)} %get-tuple-element.233), kind=kOutput, calls=%fused_computation.3.clone.1 | convolution fusion | flops 301989888 | bytes 12189696 | tf_op jit(solution)/shard_map/while/body/eval_jaxpr/pksb,cpkb->cps/dot_general | solution.py:23
  257.3 13.3 %gather_fusion = bf16[384,64,128]{2,1,0:T(8,128)(2,1)} fusion(bf16[64,16,128]{2,0,1:T(8,128)(2,1)S(1)} %copy.39, s32[1024]{0:T(1024)S(1)} %pad_clamp_fusion.2), kind=kCustom, calls=%fused_computation.1.clone.clone.1 | custom fusion | bytes 12584448 | tf_op jit(solution)/shard_map/while/body/eval_jaxpr/gather | solution.py:27
  270.6 5.9 %convolution_bitcast_fusion.4 = f32[64,96,48]{0,2,1:T(8,128)S(1)} fusion(bf16[64,96,4,128]{3,0,2,1:T(8,128)(2,1)} %bitcast.66, bf16[96,4,48,128]{3,2,1,0:T(8,128)(2,1)} %get-tuple-element.233), kind=kOutput, calls=%fused_computation.2.clone.1 | convolution fusion | flops 301989888 | bytes 12189696 | tf_op jit(solution)/shard_map/while/body/eval_jaxpr/pksb,cpkb->cps/dot_general | solution.py:26
  278.6 13.3 %gather_fusion.1 = bf16[384,64,128]{2,1,0:T(8,128)(2,1)} fusion(bf16[64,16,128]{2,0,1:T(8,128)(2,1)S(1)} %copy.41, s32[1024]{0:T(1024)S(1)} %pad_clamp_fusion.2), kind=kCustom, calls=%fused_computation.clone.clone.1 | custom fusion | bytes 12584448 | tf_op jit(solution)/shard_map/while/body/eval_jaxpr/gather | solution.py:24
  291.9 5.9 %convolution_bitcast_fusion.5 = f32[64,96,48]{0,2,1:T(8,128)S(1)} fusion(bf16[64,96,4,128]{3,0,2,1:T(8,128)(2,1)} %bitcast.65, bf16[96,4,48,128]{3,2,1,0:T(8,128)(2,1)} %get-tuple-element.233), kind=kOutput, calls=%fused_computation.3.clone.1 | convolution fusion | flops 301989888 | bytes 12189696 | tf_op jit(solution)/shard_map/while/body/eval_jaxpr/pksb,cpkb->cps/dot_general | solution.py:23
  303.6 13.3 %gather_fusion = bf16[384,64,128]{2,1,0:T(8,128)(2,1)} fusion(bf16[64,16,128]{2,0,1:T(8,128)(2,1)S(1)} %copy.39, s32[1024]{0:T(1024)S(1)} %pad_clamp_fusion.2), kind=kCustom, calls=%fused_computation.1.clone.clone.1 | custom fusion | bytes 12584448 | tf_op jit(solution)/shard_map/while/body/eval_jaxpr/gather | solution.py:27
  316.9 5.9 %convolution_bitcast_fusion.4 = f32[64,96,48]{0,2,1:T(8,128)S(1)} fusion(bf16[64,96,4,128]{3,0,2,1:T(8,128)(2,1)} %bitcast.66, bf16[96,4,48,128]{3,2,1,0:T(8,128)(2,1)} %get-tuple-element.233), kind=kOutput, calls=%fused_computation.2.clone.1 | convolution fusion | flops 301989888 | bytes 12189696 | tf_op jit(solution)/shard_map/while/body/eval_jaxpr/pksb,cpkb->cps/dot_general | solution.py:26
  325.0 13.3 %gather_fusion.1 = bf16[384,64,128]{2,1,0:T(8,128)(2,1)} fusion(bf16[64,16,128]{2,0,1:T(8,128)(2,1)S(1)} %copy.41, s32[1024]{0:T(1024)S(1)} %pad_clamp_fusion.2), kind=kCustom, calls=%fused_computation.clone.clone.1 | custom fusion | bytes 12584448 | tf_op jit(solution)/shard_map/while/body/eval_jaxpr/gather | solution.py:24
  338.3 5.9 %convolution_bitcast_fusion.5 = f32[64,96,48]{0,2,1:T(8,128)S(1)} fusion(bf16[64,96,4,128]{3,0,2,1:T(8,128)(2,1)} %bitcast.65, bf16[96,4,48,128]{3,2,1,0:T(8,128)(2,1)} %get-tuple-element.233), kind=kOutput, calls=%fused_computation.3.clone.1 | convolution fusion | flops 301989888 | bytes 12189696 | tf_op jit(solution)/shard_map/while/body/eval_jaxpr/pksb,cpkb->cps/dot_general | solution.py:23
  348.7 89.7 %all-reduce = f32[3072]{0:T(1024)S(1)} all-reduce(f32[3072]{0:T(1024)S(1)} %bitcast.73), channel_id=2, replica_groups=mesh['freq'=16,'patch'=32] {'patch'}, use_global_device_ids=true, to_apply=%region_3.0.clone | all-reduce | flops 3072 | bytes 24576
  438.5 40.8 %psum.7 = f32[96]{0:T(128)} all-reduce(f32[96]{0:T(128)S(1)} %dynamic-slice.1), channel_id=1, replica_groups=mesh['freq'=16,'patch'=32] {'freq'}, use_global_device_ids=true, to_apply=%region_4.0 | all-reduce | flops 96 | bytes 768 | tf_op jit(solution)/shard_map/psum | solution.py:63
  (66 shorter events, 36.9 us)
Async XLA Ops:
  6.5 86.3 %all-gather.3.cloned.1.call-start = ((), (), s32[]{:S(2)}) async-start(), calls=%async_computation.2 | async-start | bytes 1081344 | tf_op jit(solution)/shard_map/all_gather | solution.py:53
  21.8 141.0 %all-gather.5.cloned.1.call-start = ((), (), s32[]{:S(2)}) async-start(), calls=%async_computation.3 | async-start | bytes 1081344 | tf_op jit(solution)/shard_map/all_gather | solution.py:54
  162.8 185.3 %copy-start = (s32[96]{0:T(128)S(1)}, s32[96]{0:T(128)}, u32[]{:S(2)}) copy-start(s32[96]{0:T(128)} %param.15) | copy-start | bytes 1156
Sparse Core Ops, SparseCore 0:
  22.0 70.8 all-gather.2
  95.0 67.8 all-gather.4
where the time goes:
time: 487 us; the launch traced here: 486 us
  blocking collectives  156 us (32%)
  local copies, waits for them, and re-layouts  133 us (27%)
  waiting for transfers between devices  119 us (24%)
  matrix products  47.9 us (10%)
  other arithmetic  16.3 us (3%)
  between operations  14.1 us (3%)
    unnamed x1, blocking collectives  89.7 us
    all_gather x1, waiting for transfers between devices, body(): lax.all_gather(regrouped[1], 'patch', axis=0, tiled=True)  70 us
    gather x4, local copies, waits for them, and re-layouts, one(): adjo[:, blocks, :]  53.2 us
    gather x4, local copies, waits for them, and re-layouts, one(): resp[:, blocks, :]  53.2 us
    all_gather x1, waiting for transfers between devices, body(): lax.all_gather(regrouped[0], 'patch', axis=0, tiled=True)  48.6 us
    psum x1, blocking collectives, body(): return lax.psum(mine, 'freq')  40.8 us
    dot_general x4, matrix products, one(): jnp.einsum('pksb,cpkb->cps', masked, adjo[:, blocks, :], preferred_elemen...  23.7 us
    dot_general x4, matrix products, one(): jnp.einsum('pksb,cpkb->cps', masked, resp[:, blocks, :], preferred_elemen...  23.7 us
  transfers between devices with their start and end apart: 2, of which 2 were waited for; matrix products, arithmetic and copies ran while one was open for 2% of the time, Pallas kernels for 0%

commit v1 on v0

--- a/solution.py
+++ b/solution.py
@@ -1,8 +1,25 @@
+import functools
 import math
 import jax
 import jax.numpy as jnp
 from jax import lax
 from jax.sharding import PartitionSpec as P
+
+
+def wrap_results(own_rows, named_axis):
+    v_now = jnp.concatenate(
+        lax.all_to_all(
+            jnp.stack(tuple((own_rows for _ in range(lax.psum(1, axis_name=named_axis)))), 0),
+            axis_name=named_axis,
+            split_axis=0,
+            concat_axis=0,
+        ),
+        0,
+    )
+    return v_now
+
+
+push_cycles_on_mesh = functools.partial(wrap_results, named_axis="patch")
 
 
 def strain_terms(total, masked, blocks, resp_piece, adjo_piece, width):
@@ -51,7 +68,7 @@
         masked,
         block_lists,
         lax.all_gather(regrouped[0], "patch", axis=0, tiled=True),
-        lax.all_gather(regrouped[1], "patch", axis=0, tiled=True),
+        push_cycles_on_mesh(regrouped[1]),
         width,
     )
     terms = terms * (samples * freqs) ** (-0.5)

time: 487 us -> 453 us (0.930)
  the two profiles are of different devices: /device:TPU:32 before, /device:TPU:2 now
where the time goes in v1:
time: 453 us; the launch traced here: 452 us
  blocking collectives  146 us (32%)
  local copies, waits for them, and re-layouts  134 us (30%)
  waiting for transfers between devices  75.8 us (17%)
  matrix products  47.9 us (11%)
  starting transfers between devices  18.6 us (4%)
  other arithmetic  16.3 us (4%)
  between operations  14 us (3%)
    unnamed x1, blocking collectives  93.3 us
    all_gather x1, waiting for transfers between devices, body(): lax.all_gather(regrouped[0], 'patch', axis=0, tiled=True)  69.5 us
    gather x4, local copies, waits for them, and re-layouts, one(): adjo[:, blocks, :]  53.2 us
    gather x4, local copies, waits for them, and re-layouts, one(): resp[:, blocks, :]  53.2 us
    psum x1, blocking collectives, body(): return lax.psum(mine, 'freq')  37 us
    dot_general x4, matrix products, one(): jnp.einsum('pksb,cpkb->cps', masked, adjo[:, blocks, :], preferred_elemen...  23.7 us
    dot_general x4, matrix products, one(): jnp.einsum('pksb,cpkb->cps', masked, resp[:, blocks, :], preferred_elemen...  23.7 us
    all_to_all x1, blocking collectives, body(): lax.all_to_all(adjoints, 'freq', split_axis=0, concat_axis=2, tiled=True)  15.5 us
  transfers between devices with their start and end apart: 3, of which 2 were waited for; matrix products, arithmetic and copies ran while one was open for 2% of the time, Pallas kernels for 0%

profile of v1, /device:TPU:2, one launch (start us, length us, event | category | flops | bytes accessed | tf_op | source)
XLA Modules:
  0.0 452.4 jit_solution(2360980050922202536)
XLA Ops:
  6.5 15.5 %all_to_all.38 = bf16[64,2,128]{2,1,0:T(2,128)(2,1)S(1)} all-to-all(bf16[64,2,128]{2,1,0:T(2,128)(2,1)} %param.10), channel_id=1, replica_groups=mesh['freq'=16,'patch'=32] {'freq'}, dimensions={0} | all-to-all | bytes 65536 | tf_op jit(solution)/shard_map/all_to_all | solution.py:64
  26.8 6.3 %all-to-all-done = bf16[64,2,128]{2,1,0:T(2,128)(2,1)S(1)} async-done(((bf16[64,2,128]{2,1,0:T(2,128)(2,1)}), bf16[64,2,128]{2,1,0:T(2,128)(2,1)S(1)}, u32[]{:S(2)}, u32[]{:S(2)}) %all-to-all-start) | async-done | bytes 32800 | tf_op jit(solution)/shard_map/all_to_all | solution.py:63
  35.0 13.8 %all-to-all-start.2 = ((bf16[32,4,2,2048]{3,2,1,0:T(2,128)(2,1)}), bf16[32,4,2,2048]{3,2,1,0:T(2,128)(2,1)}, u32[]{:S(2)}, u32[]{:S(2)}) async-start(bf16[32,4,2,2048]{3,2,1,0:T(2,128)(2,1)} %stack.5), calls=%async_computation.2 | async-start | bytes 2097152 | tf_op jit(solution)/shard_map/all_to_all | solution.py:11
  53.9 6.3 %broadcast_multiply_fusion = bf16[96,4,48,128]{3,2,1,0:T(8,128)(2,1)} fusion(bf16[96,4,48,128]{3,2,1,0:T(8,128)(2,1)} %param.11, bf16[96,4,48]{2,1,0:T(4,128)(2,1)S(1)} %and_convert_fusion), kind=kLoop, calls=%fused_computation.14 | loop fusion | flops 2359296 | bytes 9474048 | tf_op jit(solution)/shard_map/mul | solution.py:59
  60.1 69.5 %all-gather.2.cloned.1.call-done = bf16[128,2,2048]{2,1,0:T(2,128)(2,1)} async-done(((bf16[4,2,2048]{2,1,0:T(2,128)(2,1)}), bf16[128,2,2048]{2,1,0:T(2,128)(2,1)}) %all-gather.2.cloned.1.call-update) | async-done | bytes 1048592 | tf_op jit(solution)/shard_map/all_gather | solution.py:70
  129.6 185.0 %while.14 = (s32[]{:T(128)}, f32[96]{0:T(128)S(1)}, bf16[128,2,2048]{2,1,0:T(2,128)(2,1)}, s32[96,4]{1,0:T(8,128)S(1)}, bf16[96,4,48,128]{3,2,1,0:T(8,128)(2,1)}...) while((s32[]{:T(128)}, f32[96]{0:T(128)S(1)}, ...), condition=%wide.region_2.0_spmd.clone, body=%wide.region_0.0_spmd.clone.sunk | while | flops 604571840 | bytes 59785376 | solution.py:51
  131.4 13.3 %gather_fusion = bf16[384,64,128]{2,1,0:T(8,128)(2,1)} fusion(bf16[64,16,128]{2,0,1:T(8,128)(2,1)S(1)} %copy.38, s32[1024]{0:T(1024)S(1)} %pad_clamp_fusion.2), kind=kCustom, calls=%fused_computation.1.clone.clone.1 | custom fusion | bytes 12584448 | tf_op jit(solution)/shard_map/while/body/eval_jaxpr/gather | solution.py:44
  144.7 5.9 %convolution_bitcast_fusion.4 = f32[64,96,48]{0,2,1:T(8,128)S(1)} fusion(bf16[64,96,4,128]{3,0,2,1:T(8,128)(2,1)} %bitcast.67, bf16[96,4,48,128]{3,2,1,0:T(8,128)(2,1)} %get-tuple-element.233), kind=kOutput, calls=%fused_computation.2.clone.1 | convolution fusion | flops 301989888 | bytes 12189696 | tf_op jit(solution)/shard_map/while/body/eval_jaxpr/pksb,cpkb->cps/dot_general | solution.py:43
  152.7 13.3 %gather_fusion.1 = bf16[384,64,128]{2,1,0:T(8,128)(2,1)} fusion(bf16[64,16,128]{2,0,1:T(8,128)(2,1)S(1)} %copy.40, s32[1024]{0:T(1024)S(1)} %pad_clamp_fusion.2), kind=kCustom, calls=%fused_computation.clone.clone.1 | custom fusion | bytes 12584448 | tf_op jit(solution)/shard_map/while/body/eval_jaxpr/gather | solution.py:41
  166.0 5.9 %convolution_bitcast_fusion.5 = f32[64,96,48]{0,2,1:T(8,128)S(1)} fusion(bf16[64,96,4,128]{3,0,2,1:T(8,128)(2,1)} %bitcast.66, bf16[96,4,48,128]{3,2,1,0:T(8,128)(2,1)} %get-tuple-element.233), kind=kOutput, calls=%fused_computation.3.clone.1 | convolution fusion | flops 301989888 | bytes 12189696 | tf_op jit(solution)/shard_map/while/body/eval_jaxpr/pksb,cpkb->cps/dot_general | solution.py:40
  177.7 13.3 %gather_fusion = bf16[384,64,128]{2,1,0:T(8,128)(2,1)} fusion(bf16[64,16,128]{2,0,1:T(8,128)(2,1)S(1)} %copy.38, s32[1024]{0:T(1024)S(1)} %pad_clamp_fusion.2), kind=kCustom, calls=%fused_computation.1.clone.clone.1 | custom fusion | bytes 12584448 | tf_op jit(solution)/shard_map/while/body/eval_jaxpr/gather | solution.py:44
  191.0 5.9 %convolution_bitcast_fusion.4 = f32[64,96,48]{0,2,1:T(8,128)S(1)} fusion(bf16[64,96,4,128]{3,0,2,1:T(8,128)(2,1)} %bitcast.67, bf16[96,4,48,128]{3,2,1,0:T(8,128)(2,1)} %get-tuple-element.233), kind=kOutput, calls=%fused_computation.2.clone.1 | convolution fusion | flops 301989888 | bytes 12189696 | tf_op jit(solution)/shard_map/while/body/eval_jaxpr/pksb,cpkb->cps/dot_general | solution.py:43
  199.0 13.3 %gather_fusion.1 = bf16[384,64,128]{2,1,0:T(8,128)(2,1)} fusion(bf16[64,16,128]{2,0,1:T(8,128)(2,1)S(1)} %copy.40, s32[1024]{0:T(1024)S(1)} %pad_clamp_fusion.2), kind=kCustom, calls=%fused_computation.clone.clone.1 | custom fusion | bytes 12584448 | tf_op jit(solution)/shard_map/while/body/eval_jaxpr/gather | solution.py:41
  212.3 5.9 %convolution_bitcast_fusion.5 = f32[64,96,48]{0,2,1:T(8,128)S(1)} fusion(bf16[64,96,4,128]{3,0,2,1:T(8,128)(2,1)} %bitcast.66, bf16[96,4,48,128]{3,2,1,0:T(8,128)(2,1)} %get-tuple-element.233), kind=kOutput, calls=%fused_computation.3.clone.1 | convolution fusion | flops 301989888 | bytes 12189696 | tf_op jit(solution)/shard_map/while/body/eval_jaxpr/pksb,cpkb->cps/dot_general | solution.py:40
  223.9 13.3 %gather_fusion = bf16[384,64,128]{2,1,0:T(8,128)(2,1)} fusion(bf16[64,16,128]{2,0,1:T(8,128)(2,1)S(1)} %copy.38, s32[1024]{0:T(1024)S(1)} %pad_clamp_fusion.2), kind=kCustom, calls=%fused_computation.1.clone.clone.1 | custom fusion | bytes 12584448 | tf_op jit(solution)/shard_map/while/body/eval_jaxpr/gather | solution.py:44
  237.2 5.9 %convolution_bitcast_fusion.4 = f32[64,96,48]{0,2,1:T(8,128)S(1)} fusion(bf16[64,96,4,128]{3,0,2,1:T(8,128)(2,1)} %bitcast.67, bf16[96,4,48,128]{3,2,1,0:T(8,128)(2,1)} %get-tuple-element.233), kind=kOutput, calls=%fused_computation.2.clone.1 | convolution fusion | flops 301989888 | bytes 12189696 | tf_op jit(solution)/shard_map/while/body/eval_jaxpr/pksb,cpkb->cps/dot_general | solution.py:43
  245.3 13.3 %gather_fusion.1 = bf16[384,64,128]{2,1,0:T(8,128)(2,1)} fusion(bf16[64,16,128]{2,0,1:T(8,128)(2,1)S(1)} %copy.40, s32[1024]{0:T(1024)S(1)} %pad_clamp_fusion.2), kind=kCustom, calls=%fused_computation.clone.clone.1 | custom fusion | bytes 12584448 | tf_op jit(solution)/shard_map/while/body/eval_jaxpr/gather | solution.py:41
  258.6 5.9 %convolution_bitcast_fusion.5 = f32[64,96,48]{0,2,1:T(8,128)S(1)} fusion(bf16[64,96,4,128]{3,0,2,1:T(8,128)(2,1)} %bitcast.66, bf16[96,4,48,128]{3,2,1,0:T(8,128)(2,1)} %get-tuple-element.233), kind=kOutput, calls=%fused_computation.3.clone.1 | convolution fusion | flops 301989888 | bytes 12189696 | tf_op jit(solution)/shard_map/while/body/eval_jaxpr/pksb,cpkb->cps/dot_general | solution.py:40
  270.2 13.3 %gather_fusion = bf16[384,64,128]{2,1,0:T(8,128)(2,1)} fusion(bf16[64,16,128]{2,0,1:T(8,128)(2,1)S(1)} %copy.38, s32[1024]{0:T(1024)S(1)} %pad_clamp_fusion.2), kind=kCustom, calls=%fused_computation.1.clone.clone.1 | custom fusion | bytes 12584448 | tf_op jit(solution)/shard_map/while/body/eval_jaxpr/gather | solution.py:44
  283.5 5.9 %convolution_bitcast_fusion.4 = f32[64,96,48]{0,2,1:T(8,128)S(1)} fusion(bf16[64,96,4,128]{3,0,2,1:T(8,128)(2,1)} %bitcast.67, bf16[96,4,48,128]{3,2,1,0:T(8,128)(2,1)} %get-tuple-element.233), kind=kOutput, calls=%fused_computation.2.clone.1 | convolution fusion | flops 301989888 | bytes 12189696 | tf_op jit(solution)/shard_map/while/body/eval_jaxpr/pksb,cpkb->cps/dot_general | solution.py:43
  291.5 13.3 %gather_fusion.1 = bf16[384,64,128]{2,1,0:T(8,128)(2,1)} fusion(bf16[64,16,128]{2,0,1:T(8,128)(2,1)S(1)} %copy.40, s32[1024]{0:T(1024)S(1)} %pad_clamp_fusion.2), kind=kCustom, calls=%fused_computation.clone.clone.1 | custom fusion | bytes 12584448 | tf_op jit(solution)/shard_map/while/body/eval_jaxpr/gather | solution.py:41
  304.8 5.9 %convolution_bitcast_fusion.5 = f32[64,96,48]{0,2,1:T(8,128)S(1)} fusion(bf16[64,96,4,128]{3,0,2,1:T(8,128)(2,1)} %bitcast.66, bf16[96,4,48,128]{3,2,1,0:T(8,128)(2,1)} %get-tuple-element.233), kind=kOutput, calls=%fused_computation.3.clone.1 | convolution fusion | flops 301989888 | bytes 12189696 | tf_op jit(solution)/shard_map/while/body/eval_jaxpr/pksb,cpkb->cps/dot_general | solution.py:40
  315.2 93.3 %all-reduce = f32[3072]{0:T(1024)S(1)} all-reduce(f32[3072]{0:T(1024)S(1)} %bitcast.74), channel_id=2, replica_groups=mesh['freq'=16,'patch'=32] {'patch'}, use_global_device_ids=true, to_apply=%region_3.0.clone | all-reduce | flops 3072 | bytes 24576
  408.6 37.0 %psum.7 = f32[96]{0:T(128)} all-reduce(f32[96]{0:T(128)S(1)} %dynamic-slice.1), channel_id=1, replica_groups=mesh['freq'=16,'patch'=32] {'freq'}, use_global_device_ids=true, to_apply=%region_4.0 | all-reduce | flops 96 | bytes 768 | tf_op jit(solution)/shard_map/psum | solution.py:80
  (67 shorter events, 42.7 us)
Async XLA Ops:
  22.0 11.0 %all-to-all-start = ((bf16[64,2,128]{2,1,0:T(2,128)(2,1)}), bf16[64,2,128]{2,1,0:T(2,128)(2,1)S(1)}, u32[]{:S(2)}, u32[]{:S(2)}) async-start(bf16[64,2,128]{2,1,0:T(2,128)(2,1)} %param.9), calls=%async_computation | async-start | bytes 65536 | tf_op jit(solution)/shard_map/all_to_all | solution.py:63
  35.0 94.6 %all-to-all-start.2 = ((bf16[32,4,2,2048]{3,2,1,0:T(2,128)(2,1)}), bf16[32,4,2,2048]{3,2,1,0:T(2,128)(2,1)}, u32[]{:S(2)}, u32[]{:S(2)}) async-start(bf16[32,4,2,2048]{3,2,1,0:T(2,128)(2,1)} %stack.5), calls=%async_computation.2 | async-start | bytes 2097152 | tf_op jit(solution)/shard_map/all_to_all | solution.py:11
  48.8 80.8 %all-gather.2.cloned.1.call-start = ((), (), s32[]{:S(2)}) async-start(), calls=%async_computation.3 | async-start | bytes 1081344 | tf_op jit(solution)/shard_map/all_gather | solution.py:70
  129.6 185.1 %copy-start = (s32[96]{0:T(128)S(1)}, s32[96]{0:T(128)}, u32[]{:S(2)}) copy-start(s32[96]{0:T(128)} %param.15) | copy-start | bytes 1156
Sparse Core Ops, SparseCore 0:
  51.8 77.7 all-gather.1
